TPU v7x, 32 devices: a whole 2x2x4 slice. The times are simulated.
32 devices in a mesh: groups: 2 (over x), space: 16 (over z, y, core).
Axes of the slice: x: 2, y: 2, z: 4, core: 2. Of those that a mesh axis runs over, the one named last changes fastest.
Arguments:
- mol_feats: bfloat16 [8192, 512], P(('groups', 'space')), parts along dimension 0, may hold values from -6 to 6
- w_src: bfloat16 [512, 512], replicated, may hold values from -0.25 to 0.25
- w_dst: bfloat16 [512, 512], replicated, may hold values from -0.25 to 0.25
- w_out: bfloat16 [512, 529], replicated, may hold values from -0.25 to 0.25
- grad_blocks: bfloat16 [16, 32, 128, 529], P('space', 'groups'), parts along dimension 1, may hold values from -6 to 6
- edge_src: int32 [65536], P(('groups', 'space')), parts along dimension 0, may hold values from 0 to 255
- edge_dst: int32 [65536], P(('groups', 'space')), parts along dimension 0, may hold values from 0 to 383
- edge_live: int32 [65536], P(('groups', 'space')), parts along dimension 0, may hold values from 0 to 1, as said below
Outputs:
- feature_grad: float32 [8192, 512], P(('groups', 'space')), parts along dimension 0
- src_weight_grad: float32 [1024, 512], P(('groups', 'space')), parts along dimension 0
- dst_weight_grad: float32 [1024, 512], P(('groups', 'space')), parts along dimension 0
- out_weight_grad: float32 [1024, 529], P(('groups', 'space')), parts along dimension 0
There are 2 independent parts, one for each index of `groups`. A program takes and returns all parts, laid end to end along the dimension named above; an argument that names none is the same for every part. Nothing has to cross between parts.
Inputs may be any that keep to these rules, and one draw needn't show every extreme that they name: `edge_live`: on every slab the live slots of each owner come first among its 128 slots, and the slab's own blocks fill all 128 of theirs. Any other owner has at most 64 live slots for a slab, and on every slab some other owner has exactly 64. `edge_dst`: index into the slab's molecules extended by 64 molecules of the slab below (first) and 64 of the slab above (last), periodic.
All inputs are finite; a program needn't handle non-finite values.
Results may differ from a plain program's by a relative error of at most 0.0029.
Values may be sent and summed in bfloat16 or wider, within the bound.
A program may use at most 64 MiB of HBM per device.

v0:
```python
import jax
import jax.numpy as jnp
from jax import lax
from jax.sharding import PartitionSpec as P


def passed_along(block, axis, distance):
    devices = range(lax.axis_size(axis))
    route = [((i - distance) % len(devices), i) for i in devices]
    return lax.ppermute(block, axis, route)


def extended_2(cells, sides, width):
    for axis, dim in sides:
        count = lax.axis_size(axis)
        head = lax.slice_in_dim(cells, 0, width, axis=dim)
        tail = lax.slice_in_dim(cells, cells.shape[dim] - width, cells.shape[dim], axis=dim)
        cells = jnp.concatenate(
            [
                lax.ppermute(tail, axis, [(i, (i + 1) % count) for i in range(count)]),
                cells,
                lax.ppermute(head, axis, [((i + 1) % count, i) for i in range(count)]),
            ],
            axis=dim,
        )
    return cells


def settle_rims(wide_sum, reach):
    mols = wide_sum.shape[0] - 2 * reach
    lower = wide_sum[:reach]
    upper = wide_sum[reach + mols :]
    from_above = passed_along(lower, "space", -1)
    from_below = passed_along(upper, "space", 1)
    middle = wide_sum[reach : reach + mols]
    middle = middle.at[:reach].add(from_below)
    return middle.at[mols - reach :].add(from_above)


def column_term(left, right, factor):
    product = lax.dot_general(
        left,
        right,
        (((0,), (0,)), ((), ())),
        precision=lax.Precision.HIGHEST,
        preferred_element_type=jnp.float32,
    )
    return factor * product


def on_device(mol_feats, w_src, w_dst, w_out, grad_blocks, edge_src, edge_dst, edge_live):
    mols = mol_feats.shape[0]
    entries = w_out.shape[1]
    reach = mols // 4
    highest = lax.Precision.HIGHEST
    transposed = (((1,), (1,)), ((), ()))
    extended = extended_2(mol_feats, (("space", 0),), reach)
    proj_src = jnp.dot(mol_feats, w_src, preferred_element_type=jnp.float32)
    proj_dst = jnp.dot(extended, w_dst, preferred_element_type=jnp.float32)
    arrived = lax.all_to_all(grad_blocks, "space", split_axis=1, concat_axis=0, tiled=True)
    blocks = arrived.reshape(-1, entries)
    blocks = jnp.where(edge_live[:, None] > 0, blocks, jnp.zeros_like(blocks))
    pre = proj_src[edge_src] + proj_dst[edge_dst]
    sigma = jax.nn.sigmoid(pre)
    hidden = (pre * sigma).astype(jnp.bfloat16)
    grad_hidden = lax.dot_general(blocks, w_out, transposed, preferred_element_type=jnp.float32)
    grad_pre = (grad_hidden * sigma * (1.0 + pre * (1.0 - sigma))).astype(jnp.bfloat16)
    grad_wide = lax.optimization_barrier(grad_pre).astype(jnp.float32)
    src_sum = jax.ops.segment_sum(grad_wide, edge_src, num_segments=mols)
    dst_wide = jax.ops.segment_sum(grad_wide, edge_dst, num_segments=mols + 2 * reach)
    dst_total = settle_rims(dst_wide, reach)
    feature_grad = jnp.dot(src_sum, w_src.astype(jnp.float32).T, precision=highest) + jnp.dot(
        dst_total, w_dst.astype(jnp.float32).T, precision=highest
    )
    factor = float(edge_src.shape[0] * lax.axis_size("space")) ** (-0.5)
    feats_wide = mol_feats.astype(jnp.float32)
    ext_wide = extended.astype(jnp.float32)
    src_weight_grad = lax.psum_scatter(
        column_term(feats_wide, src_sum, factor), "space", scatter_dimension=0, tiled=True
    )
    dst_weight_grad = lax.psum_scatter(
        column_term(ext_wide, dst_wide, factor), "space", scatter_dimension=0, tiled=True
    )
    product = lax.dot_general(
        hidden, blocks, (((0,), (0,)), ((), ())), preferred_element_type=jnp.float32
    )
    out_weight_grad = lax.psum_scatter(factor * product, "space", scatter_dimension=0, tiled=True)
    return (feature_grad, src_weight_grad, dst_weight_grad, out_weight_grad)


def solution(mesh):
    placed = (
        P(("groups", "space"), None),
        P(),
        P(),
        P(),
        P("space", "groups", None, None),
        P(("groups", "space")),
        P(("groups", "space")),
        P(("groups", "space")),
    )
    return jax.shard_map(
        on_device,
        mesh=mesh,
        in_specs=placed,
        out_specs=(
            P(("groups", "space"), None),
            P(("groups", "space"), None),
            P(("groups", "space"), None),
            P(("groups", "space"), None),
        ),
        check_vma=False,
    )
```

profile of v0, /device:TPU:0, one launch (start us, length us, event | category | flops | bytes accessed | tf_op | source)
XLA Modules:
  0.0 292.4 jit_solution(4587517296089946174)
XLA Ops:
  7.2 0.0 copy-start
  7.2 0.0 copy-start.4
  7.2 0.0 copy-start.10
  7.2 0.0 copy-start.11
  7.2 3.7 %copy.15 = bf16[1,16,128,529]{2,3,0,1:T(8,128)(2,1)} copy(bf16[1,16,128,529]{2,1,3,0:T(8,128)(2,1)} %param.16) | data formatting | bytes 4333568 | tf_op args[4]
  10.9 7.4 %all-to-all-start = ((bf16[1,16,128,529]{2,3,0,1:T(8,128)(2,1)}), bf16[1,16,128,529]{2,3,0,1:T(8,128)(2,1)S(1)}, u32[]{:S(2)}, u32[]{:S(2)}) async-start(bf16[1,16,128,529]{2,3,0,1:T(8,128)(2,1)} %copy.15), calls=%async_computation | async-start | bytes 4390912 | tf_op jit(solution)/shard_map/all_to_all | solution.py:60
  18.3 0.0 reduce-scatter.6.cloned.1.call-start
  18.3 0.7 fusion.20
  19.0 4.4 %collective-permute-start.1 = (bf16[64,512]{1,0:T(8,128)(2,1)}, bf16[64,512]{1,0:T(8,128)(2,1)}, u32[]{:S(2)}, u32[]{:S(2)}) collective-permute-start(bf16[64,512]{1,0:T(8,128)(2,1)} %get-tuple-element.42), channel_id=1, source_target_pairs={{1,0},{2,1},{3,2},{4,3},{5,4},{6,5},{7,6},{8,7},{9,8},{10,9},{11,1... | collective-permute-start | bytes 196616 | tf_op jit(solution)/shard_map/ppermute | solution.py:22
  23.4 1.3 fusion.21
  24.8 0.6 broadcast_compare_fusion
  25.3 8.9 %gather_fusion = f32[2048,512]{1,0:T(8,128)} fusion(f32[256,512]{1,0:T(8,128)S(1)} %fusion.21, s32[2048]{0:T(1024)S(1)} %get-tuple-element.44), kind=kCustom, calls=%fused_computation | custom fusion | bytes 8396800 | tf_op jit(solution)/shard_map/gather | solution.py:63
  34.2 26.3 %collective-permute-done = bf16[64,512]{1,0:T(8,128)(2,1)} collective-permute-done((bf16[64,512]{1,0:T(8,128)(2,1)}, bf16[64,512]{1,0:T(8,128)(2,1)}, u32[]{:S(2)}, u32[]{:S(2)}) %collective-permute-start) | collective-permute-done | bytes 65568 | tf_op jit(solution)/shard_map/ppermute | solution.py:20
  60.5 0.8 constant_dynamic-update-slice_fusion.2
  61.4 0.8 constant_dynamic-update-slice_fusion
  62.3 0.7 copy-done.8
  63.0 1.4 fusion.22
  64.4 9.0 %gather_fusion.1 = f32[2048,512]{1,0:T(8,128)} fusion(f32[384,512]{1,0:T(8,128)S(1)} %fusion.22, s32[2048]{0:T(1024)S(1)} %get-tuple-element.45), kind=kCustom, calls=%fused_computation.1 | custom fusion | bytes 8396800 | tf_op jit(solution)/shard_map/gather | solution.py:63
  73.4 0.3 copy.22
  73.7 0.0 copy-start.12
  73.7 0.4 pad.6
  74.1 0.6 copy.20
  74.7 1.4 copy-done.5
  76.1 0.3 copy-done.2
  76.5 1.5 copy-done.3
  77.9 3.1 %multiply_convert_fusion.1 = bf16[2048,512]{1,0:T(8,128)(2,1)S(1)} fusion(bf16[512,529]{0,1:T(8,128)(2,1)S(1)} %copy-done, bf16[2048,529]{0,1:T(8,128)(2,1)S(1)} %bitcast.26, pred[2048]{0:T(1024)(128)(4,1)S(1)} %copy-done.12, f32[2048,512]{1,0:T(8,128)S(1)} %copy-done.2, f32[2048,512]{1,0:T(8,128)S(1)} %copy-done.3), kind=kOutput, calls=%fused_computation.9 | convolution fusion | flops 1120962560 | bytes 13196288 | tf_op jit(solution)/shard_map/dot_general | solution.py:66
  81.0 13.2 %scatter_custom_fusion.1 = f32[384,512]{1,0:T(8,128)S(1)} fusion(s32[2048]{0:T(1024)} %param.18, bf16[2048,512]{1,0:T(8,128)(2,1)S(1)} %multiply_convert_fusion.1, f32[]{:T(128)} %constant.64.clone.1), kind=kCustom, calls=%fused_computation.4 | custom fusion | flops 2097152 | bytes 2884096 | tf_op jit(solution)/shard_map/scatter-add | solution.py:70
  94.2 3.0 %convolution_multiply_fusion = f32[512,512]{1,0:T(8,128)} fusion(bf16[384,512]{1,0:T(8,128)(2,1)} %copy-done.8, f32[384,512]{1,0:T(8,128)S(1)} %scatter_custom_fusion.1), kind=kOutput, calls=%fused_computation.16 | convolution fusion | flops 1208221696 | bytes 2228224 | tf_op jit(solution)/shard_map/dot_general | solution.py:41
  97.2 0.0 reduce-scatter.6.cloned.1.call-update
  97.3 0.0 reduce-scatter.10.cloned.1.call-start
  97.3 13.7 %scatter_custom_fusion = f32[256,512]{1,0:T(8,128)} fusion(s32[2048]{0:T(1024)} %param.17, bf16[2048,512]{1,0:T(8,128)(2,1)S(1)} %multiply_convert_fusion.1, f32[]{:T(128)} %constant.64.clone.1), kind=kCustom, calls=%fused_computation.6 | custom fusion | flops 2097152 | bytes 2621952 | tf_op jit(solution)/shard_map/scatter-add | solution.py:69
  111.0 1.7 fusion.7
  112.8 1.3 copy.18
  114.1 0.0 reduce-scatter.10.cloned.1.call-update
  114.2 0.0 copy-start.1
  114.2 0.0 copy-start.6
  114.2 0.0 reduce-scatter.8.cloned.1.call-start
  114.2 7.8 %fusion.6 = f32[512,529]{1,0:T(8,128)} fusion(bf16[2048,529]{0,1:T(8,128)(2,1)} %bitcast.27, pred[2048]{0:T(1024)(128)(4,1)S(1)} %copy-done.12, f32[2048,512]{1,0:T(8,128)} %gather_fusion, f32[2048,512]{1,0:T(8,128)} %gather_fusion.1), kind=kOutput, calls=%fused_computation.15 | convolution fusion | flops 1117039104 | bytes 11640832 | tf_op jit(solution)/shard_map/dot_general | solution.py:84
  122.0 0.0 reduce-scatter.8.cloned.1.call-update
  122.1 0.1 collective-permute-start.2
  122.2 0.6 fusion.23
  122.8 4.5 %collective-permute-start.3 = (f32[64,512]{1,0:T(8,128)S(1)}, f32[64,512]{1,0:T(8,128)S(1)}, u32[]{:S(2)}, u32[]{:S(2)}) collective-permute-start(f32[64,512]{1,0:T(8,128)S(1)} %get-tuple-element.40), channel_id=1, source_target_pairs={{1,0},{2,1},{3,2},{4,3},{5,4},{6,5},{7,6},{8,7},{9,8},{10,9},{11,1... | collective-permute-start | bytes 393224 | tf_op jit(solution)/shard_map/ppermute | solution.py:10
  127.3 1.9 collective-permute-done.2
  129.3 0.6 collective-permute-done.3
  129.9 1.4 convolution_add_fusion
  131.3 31.8 %reduce-scatter.6.cloned.1.call-done = f32[32,512]{1,0:T(8,128)} async-done(((f32[512,512]{1,0:T(8,128)}), f32[32,512]{1,0:T(8,128)}) %reduce-scatter.6.cloned.1.call-update) | async-done | bytes 65552 | tf_op jit(solution)/shard_map/reduce_scatter | solution.py:81
  163.1 61.0 %reduce-scatter.10.cloned.1.call-done = f32[32,512]{1,0:T(8,128)} async-done(((f32[512,512]{1,0:T(8,128)}), f32[32,512]{1,0:T(8,128)}) %reduce-scatter.10.cloned.1.call-update) | async-done | bytes 65552
  224.2 61.7 %reduce-scatter.8.cloned.1.call-done = f32[32,529]{1,0:T(8,128)} async-done(((f32[512,529]{1,0:T(8,128)}), f32[32,529]{1,0:T(8,128)}) %reduce-scatter.8.cloned.1.call-update) | async-done | bytes 67728 | tf_op jit(solution)/shard_map/reduce_scatter | solution.py:87
  (24 shorter events, 0.2 us)
Async XLA Ops:
  7.2 68.9 %copy-start = (bf16[512,529]{0,1:T(8,128)(2,1)S(1)}, bf16[512,529]{0,1:T(8,128)(2,1)}, u32[]{:S(2)}) copy-start(bf16[512,529]{0,1:T(8,128)(2,1)} %param.15) | copy-start | bytes 1625092
  7.2 11.1 %copy-start.4 = (bf16[256,512]{1,0:T(8,128)(2,1)S(1)}, bf16[256,512]{1,0:T(8,128)(2,1)}, u32[]{:S(2)}) copy-start(bf16[256,512]{1,0:T(8,128)(2,1)} %param.12) | copy-start | bytes 786436
  7.2 16.2 %copy-start.10 = (s32[2048]{0:T(1024)S(1)}, s32[2048]{0:T(1024)}, u32[]{:S(2)}) copy-start(s32[2048]{0:T(1024)} %param.18) | copy-start | bytes 24580
  7.2 16.2 %copy-start.11 = (s32[2048]{0:T(1024)S(1)}, s32[2048]{0:T(1024)}, u32[]{:S(2)}) copy-start(s32[2048]{0:T(1024)} %param.17) | copy-start | bytes 24580
  7.2 17.5 %copy-start.9 = (s32[2048]{0:T(1024)S(1)}, s32[2048]{0:T(1024)}, u32[]{:S(2)}) copy-start(s32[2048]{0:T(1024)} %param.19) | copy-start | bytes 24580
  10.9 62.5 %all-to-all-start = ((bf16[1,16,128,529]{2,3,0,1:T(8,128)(2,1)}), bf16[1,16,128,529]{2,3,0,1:T(8,128)(2,1)S(1)}, u32[]{:S(2)}, u32[]{:S(2)}) async-start(bf16[1,16,128,529]{2,3,0,1:T(8,128)(2,1)} %copy.15), calls=%async_computation | async-start | bytes 4390912 | tf_op jit(solution)/shard_map/all_to_all | solution.py:60
  18.3 144.8 %reduce-scatter.6.cloned.1.call-start = ((), (), s32[]{:S(2)}) async-start(), calls=%async_computation.4 | async-start | bytes 1114112 | tf_op jit(solution)/shard_map/reduce_scatter | solution.py:81
  19.0 42.4 %collective-permute-start.1 = (bf16[64,512]{1,0:T(8,128)(2,1)}, bf16[64,512]{1,0:T(8,128)(2,1)}, u32[]{:S(2)}, u32[]{:S(2)}) collective-permute-start(bf16[64,512]{1,0:T(8,128)(2,1)} %get-tuple-element.42), channel_id=1, source_target_pairs={{1,0},{2,1},{3,2},{4,3},{5,4},{6,5},{7,6},{8,7},{9,8},{10,9},{11,1... | collective-permute-start | bytes 196616 | tf_op jit(solution)/shard_map/ppermute | solution.py:22
  23.4 37.2 %collective-permute-start = (bf16[64,512]{1,0:T(8,128)(2,1)}, bf16[64,512]{1,0:T(8,128)(2,1)}, u32[]{:S(2)}, u32[]{:S(2)}) collective-permute-start(bf16[64,512]{1,0:T(8,128)(2,1)} %get-tuple-element.43), channel_id=1, source_target_pairs={{0,1},{1,2},{2,3},{3,4},{4,5},{5,6},{6,7},{7,8},{8,9},{9,10},{10,1... | collective-permute-start | bytes 196616 | tf_op jit(solution)/shard_map/ppermute | solution.py:20
  62.3 0.7 copy-start.8
  73.7 2.8 copy-start.2
  73.7 4.3 %copy-start.3 = (f32[2048,512]{1,0:T(8,128)S(1)}, f32[2048,512]{1,0:T(8,128)}, u32[]{:S(2)}) copy-start(f32[2048,512]{1,0:T(8,128)} %gather_fusion.1) | copy-start | bytes 12582916
  73.7 4.2 %copy-start.12 = (pred[2048]{0:T(1024)(128)(4,1)S(1)}, pred[2048]{0:T(1024)(128)(4,1)}, u32[]{:S(2)}) copy-start(pred[2048]{0:T(1024)(128)(4,1)} %broadcast_compare_fusion) | copy-start | bytes 6148
  74.7 1.4 copy-start.5
  97.3 126.9 %reduce-scatter.10.cloned.1.call-start = ((), (), s32[]{:S(2)}) async-start(), calls=%async_computation.6 | async-start | bytes 1114112
  114.2 8.0 %copy-start.1 = (f32[256,512]{1,0:T(8,128)S(1)}, f32[256,512]{1,0:T(8,128)}, u32[]{:S(2)}) copy-start(f32[256,512]{1,0:T(8,128)} %scatter_custom_fusion) | copy-start | bytes 1572868
  114.2 8.0 %copy-start.6 = (bf16[512,512]{1,0:T(8,128)(2,1)S(1)}, bf16[512,512]{1,0:T(8,128)(2,1)}, u32[]{:S(2)}) copy-start(bf16[512,512]{1,0:T(8,128)(2,1)} %param.13) | copy-start | bytes 1572868
  114.2 171.7 %reduce-scatter.8.cloned.1.call-start = ((), (), s32[]{:S(2)}) async-start(), calls=%async_computation.5 | async-start | bytes 1392640 | tf_op jit(solution)/shard_map/reduce_scatter | solution.py:87
  122.0 7.8 %copy-start.7 = (bf16[512,512]{1,0:T(8,128)(2,1)S(1)}, bf16[512,512]{1,0:T(8,128)(2,1)}, u32[]{:S(2)}) copy-start(bf16[512,512]{1,0:T(8,128)(2,1)} %param.14) | copy-start | bytes 1572868
  122.1 7.1 %collective-permute-start.2 = (f32[64,512]{1,0:T(8,128)S(1)}, f32[64,512]{1,0:T(8,128)S(1)}, u32[]{:S(2)}, u32[]{:S(2)}) collective-permute-start(f32[64,512]{1,0:T(8,128)S(1)} %get-tuple-element.41), channel_id=1, source_target_pairs={{15,0},{0,1},{1,2},{2,3},{3,4},{4,5},{5,6},{6,7},{7,8},{8,9},{9,10... | collective-permute-start | bytes 393224 | tf_op jit(solution)/shard_map/ppermute | solution.py:10
  122.8 7.0 %collective-permute-start.3 = (f32[64,512]{1,0:T(8,128)S(1)}, f32[64,512]{1,0:T(8,128)S(1)}, u32[]{:S(2)}, u32[]{:S(2)}) collective-permute-start(f32[64,512]{1,0:T(8,128)S(1)} %get-tuple-element.40), channel_id=1, source_target_pairs={{1,0},{2,1},{3,2},{4,3},{5,4},{6,5},{7,6},{8,7},{9,8},{10,9},{11,1... | collective-permute-start | bytes 393224 | tf_op jit(solution)/shard_map/ppermute | solution.py:10
Sparse Core Ops, SparseCore 0:
  97.4 65.6 reduce-scatter.5
  167.7 56.3 reduce-scatter.9
  228.4 57.4 reduce-scatter.7
where the time goes:
time: 293 us; the launch traced here: 292 us
  waiting for transfers between devices  183 us (62%)
  local copies, waits for them, and re-layouts  30.6 us (10%)
  other arithmetic  27.5 us (9%)
  matrix products  20.5 us (7%)
  starting transfers between devices  16.4 us (6%)
  between operations  14 us (5%)
    reduce_scatter x1, waiting for transfers between devices, on_device(): lax.psum_scatter(factor * product, 'space', scatter_dimension=0, tiled=True)  61.7 us
    unnamed x4, waiting for transfers between devices  61.1 us
    reduce_scatter x1, waiting for transfers between devices, on_device(): lax.psum_scatter(column_term(ext_wide, dst_wide, factor), 'space', scatte...  31.8 us
    ppermute x1, waiting for transfers between devices, extended_2(): lax.ppermute(tail, axis, [(i, (i + 1) % count) for i in range(count)])  26.3 us
    gather x2, local copies, waits for them, and re-layouts, on_device(): pre = proj_src[edge_src] + proj_dst[edge_dst]  17.9 us
    scatter-add x1, other arithmetic, on_device(): src_sum = jax.ops.segment_sum(grad_wide, edge_src, num_segments=mols)  13.7 us
    scatter-add x1, other arithmetic, on_device(): jax.ops.segment_sum(grad_wide, edge_dst, num_segments=mols + 2 * reach)  13.2 us
    unnamed x32, local copies, waits for them, and re-layouts  10.9 us
  transfers between devices with their start and end apart: 8, of which 6 were waited for; matrix products, arithmetic and copies ran while one was open for 17% of the time, Pallas kernels for 0%

commit v1 on v0

v1 whole, which is shorter than its diff:
```python
import functools

import jax
import jax.numpy as jnp
from jax import lax
from jax.experimental import pallas as pl
from jax.experimental.pallas import tpu as pltpu
from jax.sharding import PartitionSpec as P

MESH = pl.DeviceIdType.MESH
F32 = jnp.float32
BF16 = jnp.bfloat16
NT = (((1,), (1,)), ((), ()))


def mm(a, b):
    return jnp.dot(a, b, preferred_element_type=F32)


def mm_nt(a, b):
    return lax.dot_general(a, b, NT, preferred_element_type=F32)


def split(x):
    high = x.astype(BF16)
    return high, (x - high.astype(F32)).astype(BF16)


def kernel(
    dims, feats, w_src, w_dst, w_out, idx, idx_own, blocks, fgrad, src_out, dst_out, out_out,
    halo, ext, own, recv, pt_hi, pt_lo, ft, oh, hid, fac, oh_own, hid_own, fac_own, sums, out_sum, back,
    block_send, block_recv, halo_send, halo_recv, back_send, back_recv, own_sem, *rs,
):
    n, half, mols, reach, factor, fused = dims
    quarter = n // 4
    chunk = quarter * half
    me = lax.axis_index("space")
    above = lax.rem(me + 1, n)
    below = lax.rem(me + n - 1, n)

    barrier = pltpu.get_barrier_semaphore()

    @pl.loop(1, n)
    def _(k):
        pl.semaphore_signal(barrier, inc=1, device_id={"space": lax.rem(me + k, n)}, device_id_type=MESH)

    local = pltpu.make_async_copy(blocks.at[0, me], own, own_sem)
    local.start()
    pl.semaphore_wait(barrier, n - 1)

    def remote(src, dst, send, arrive, device):
        return pltpu.make_async_remote_copy(
            src_ref=src, dst_ref=dst, send_sem=send, recv_sem=arrive,
            device_id={"space": device}, device_id_type=MESH,
        )

    def block_copy(source_slot, target):
        return remote(
            blocks.at[0, target, pl.ds(0, half)], recv.at[source_slot],
            block_send.at[target], block_recv.at[source_slot], target,
        )

    up = remote(feats.at[pl.ds(mols - reach, reach)], halo.at[0], halo_send.at[0], halo_recv.at[0], above)
    down = remote(feats.at[pl.ds(0, reach)], halo.at[1], halo_send.at[1], halo_recv.at[1], below)
    up.start()
    down.start()

    @pl.loop(1, n)
    def _(k):
        block_copy(me, lax.rem(me + k, n)).start()

    recv[me] = jnp.zeros(recv.shape[1:], BF16)
    ext[0:mols] = feats[...]
    pt = mm(feats[...], w_src[...]).T
    high, low = split(pt)
    pt_hi[:, 0:mols] = high
    pt_lo[:, 0:mols] = low
    up.wait()
    down.wait()
    ext[mols : mols + reach] = halo[0]
    ext[mols + reach : mols + 2 * reach] = halo[1]
    pt = mm(ext[...], w_dst[...]).T
    high, low = split(pt)
    pt_hi[:, mols:] = high
    pt_lo[:, mols:] = low
    ft[...] = ext[...].astype(F32).T.astype(BF16)

    def one_hot(ids, count):
        return (lax.broadcasted_iota(jnp.int32, (count, ids.shape[1]), 0) == ids).astype(F32).astype(BF16)

    def ahead(ids, oh_ref, hid_ref, fac_ref):
        oh_ref[0:mols] = one_hot(ids[0:1], mols)
        oh_ref[mols:] = one_hot(ids[1:2], mols + 2 * reach)
        pre = mm(pt_hi[...], oh_ref[...]) + mm(pt_lo[...], oh_ref[...])
        sigma = jax.nn.sigmoid(pre)
        hid_ref[...] = (pre * sigma).astype(BF16)
        fac_ref[...] = sigma * (1.0 + pre * (1.0 - sigma))

    def terms(g, oh_ref, hid_ref, fac_ref):
        dpre = (mm_nt(w_out[...], g) * fac_ref[...]).astype(BF16)
        return mm_nt(oh_ref[...], dpre), mm(hid_ref[...], g)

    ahead(idx_own[...], oh_own, hid_own, fac_own)
    local.wait()
    s, o = terms(own[...], oh_own, hid_own, fac_own)
    sums[...] = s
    out_sum[...] = o

    @pl.loop(0, 4)
    def _(c):
        ahead(idx[c], oh.at[c], hid.at[c], fac.at[c])

    @pl.loop(0, 4)
    def _(k):
        c = lax.rem(me // quarter + k, 4)

        @pl.loop(0, quarter)
        def _(j):
            owner = c * quarter + j

            @pl.when(owner != me)
            def _():
                block_copy(owner, lax.rem(owner + 0, n)).wait_recv()

        g = recv[pl.ds(c * quarter, quarter)].reshape(chunk, recv.shape[2])
        s, o = terms(g, oh.at[c], hid.at[c], fac.at[c])
        sums[...] += s
        out_sum[...] += o

    give_down = remote(sums.at[pl.ds(2 * mols, reach)], back.at[1], back_send.at[0], back_recv.at[1], below)
    give_up = remote(sums.at[pl.ds(2 * mols + reach, reach)], back.at[0], back_send.at[1], back_recv.at[0], above)

    def source_grad():
        high, low = split(sums[0:mols])
        return (mm(ft[:, 0:mols], high) + mm(ft[:, 0:mols], low)) * factor

    def target_grad():
        high, low = split(sums[mols:])
        return (mm(ft[...], high) + mm(ft[...], low)) * factor

    def feature_part():
        high, low = split(sums[0:mols])
        fgrad[...] = mm_nt(high, w_src[...]) + mm_nt(low, w_src[...])

    def feature_rest():
        give_down.wait()
        give_up.wait()
        total = jnp.concatenate(
            [
                sums[mols : mols + reach] + back[0],
                sums[mols + reach : 2 * mols - reach],
                sums[2 * mols - reach : 2 * mols] + back[1],
            ],
            axis=0,
        )
        high, low = split(total)
        fgrad[...] += mm_nt(high, w_dst[...]) + mm_nt(low, w_dst[...])

    if fused:
        chains = [rs[8 * a : 8 * a + 8] for a in range(3)]
        send_a, recv_a, send_b, recv_b, send_c, recv_c = rs[24:]
        core = lax.rem(me, 2)
        row = lax.rem(me // 2, 2)
        column = me // 4
        rows = out_out.shape[0]

        def stage_a(a, value):
            full, s1, r1 = chains[a][:3]
            value = value.reshape(quarter, 2, 2, rows, value.shape[1])
            for y in range(2):
                for p in range(2):
                    full[p, y] = value[:, y, p]
            s1[...] = full[1 - core].astype(BF16)
            copy_a(a).start()

        def copy_a(a):
            return remote(chains[a][1], chains[a][2], send_a.at[a], recv_a.at[a], me + 1 - 2 * core)

        def copy_b(a):
            return remote(chains[a][4], chains[a][5], send_b.at[a], recv_b.at[a], me + 2 - 4 * row)

        def stage_b(a):
            full, s1, r1, keep, s2 = chains[a][:5]
            copy_a(a).wait()
            s2[...] = (full[core, 1 - row] + r1[1 - row].astype(F32)).astype(BF16)
            copy_b(a).start()
            keep[...] = full[core, row] + r1[row].astype(F32)

        def copy_c(a, slot, target):
            return remote(
                chains[a][6].at[target], chains[a][7].at[slot], send_c.at[a, target], recv_c.at[a, slot],
                target * 4 + lax.rem(me, 4),
            )

        def stage_c(a):
            keep, s2, r2, s3, r3 = chains[a][3:]
            copy_b(a).wait()
            total = keep[...] + r2[...].astype(F32)
            keep[...] = total
            s3[...] = total.astype(BF16)

            @pl.loop(1, quarter)
            def _(k):
                copy_c(a, column, lax.rem(column + k, quarter)).start()

        def stage_d(a, result):
            keep, s2, r2, s3, r3 = chains[a][3:]
            r3[column] = jnp.zeros(r3.shape[1:], BF16)

            @pl.loop(1, quarter)
            def _(k):
                other = lax.rem(column + k, quarter)
                copy_c(a, other, other).wait()

            total = keep[column]
            for z in range(quarter):
                total = total + r3[z].astype(F32)
            result[...] = total

        stage_a(0, out_sum[...] * factor)
        give_down.start()
        give_up.start()
        stage_a(1, source_grad())
        stage_b(0)
        stage_a(2, target_grad())
        stage_b(1)
        stage_c(0)
        stage_b(2)
        feature_part()
        stage_c(1)
        feature_rest()
        stage_c(2)
        stage_d(0, out_out)
        stage_d(1, src_out)
        stage_d(2, dst_out)
    else:
        give_down.start()
        give_up.start()
        out_out[...] = out_sum[...] * factor
        src_out[...] = source_grad()
        dst_out[...] = target_grad()
        feature_part()
        feature_rest()

    @pl.loop(1, n)
    def _(k):
        block_copy(me, lax.rem(me + k, n)).wait_send()


def on_device(mol_feats, w_src, w_dst, w_out, grad_blocks, edge_src, edge_dst, edge_live):
    mols, width = mol_feats.shape
    entries = w_out.shape[1]
    reach = mols // 4
    n = grad_blocks.shape[1]
    cap = grad_blocks.shape[2]
    half = cap // 2
    quarter = n // 4
    chunk = quarter * half
    rows = width // n
    fused = rows % 16 == 0
    factor = float(edge_src.shape[0] * n) ** (-0.5)
    me = lax.axis_index("space")

    below = edge_dst < reach
    inside = edge_dst < reach + mols
    target = jnp.where(below, edge_dst + mols, jnp.where(inside, edge_dst - reach, edge_dst))
    ids = jnp.stack([edge_src, target]).reshape(2, n, cap)
    ids = jnp.where(edge_live.reshape(1, n, cap) > 0, ids, -1)
    idx_own = lax.dynamic_index_in_dim(ids, me, 1, keepdims=False)
    own_row = lax.broadcasted_iota(jnp.int32, (2, n, half), 1) == me
    idx = jnp.where(own_row, -1, ids[:, :, :half]).reshape(2, 4, chunk).transpose(1, 0, 2)

    span = mols + 2 * reach
    count = mols + span
    vm = pltpu.VMEM
    dma = pltpu.SemaphoreType.DMA
    scratch = [
        vm((2, reach, width), BF16),
        vm((span, width), BF16),
        vm((cap, entries), BF16),
        vm((n, half, entries), BF16),
        vm((width, count), BF16),
        vm((width, count), BF16),
        vm((width, span), BF16),
        vm((4, count, chunk), BF16),
        vm((4, width, chunk), BF16),
        vm((4, width, chunk), F32),
        vm((count, cap), BF16),
        vm((width, cap), BF16),
        vm((width, cap), F32),
        vm((count, width), F32),
        vm((width, entries), F32),
        vm((2, reach, width), F32),
        dma((n,)), dma((n,)), dma((2,)), dma((2,)), dma((2,)), dma((2,)), dma(()),
    ]
    if fused:
        for columns in (entries, width, width):
            piece = (quarter, rows, columns)
            scratch += [
                vm((2, 2) + piece, F32),
                vm((2,) + piece, BF16),
                vm((2,) + piece, BF16),
                vm(piece, F32),
                vm(piece, BF16),
                vm(piece, BF16),
                vm(piece, BF16),
                vm(piece, BF16),
            ]
        scratch += [dma((3,)), dma((3,)), dma((3,)), dma((3,)), dma((3, quarter)), dma((3, quarter))]
    out_rows = rows if fused else width
    whole = pl.BlockSpec(memory_space=pltpu.VMEM)
    fgrad, src_g, dst_g, out_g = pl.pallas_call(
        functools.partial(kernel, (n, half, mols, reach, factor, fused)),
        out_shape=(
            jax.ShapeDtypeStruct((mols, width), F32),
            jax.ShapeDtypeStruct((out_rows, width), F32),
            jax.ShapeDtypeStruct((out_rows, width), F32),
            jax.ShapeDtypeStruct((out_rows, entries), F32),
        ),
        in_specs=[whole] * 6 + [pl.BlockSpec(memory_space=pl.ANY)],
        out_specs=(whole,) * 4,
        scratch_shapes=scratch,
        compiler_params=pltpu.CompilerParams(
            collective_id=0, has_side_effects=True, vmem_limit_bytes=48 * 1024 * 1024
        ),
    )(mol_feats, w_src, w_dst, w_out, idx, idx_own, grad_blocks)
    if not fused:
        src_g, dst_g, out_g = [
            lax.psum_scatter(part, "space", scatter_dimension=0, tiled=True) for part in (src_g, dst_g, out_g)
        ]
    return fgrad, src_g, dst_g, out_g


def solution(mesh):
    placed = (
        P(("groups", "space"), None),
        P(),
        P(),
        P(),
        P("space", "groups", None, None),
        P(("groups", "space")),
        P(("groups", "space")),
        P(("groups", "space")),
    )
    return jax.shard_map(
        on_device,
        mesh=mesh,
        in_specs=placed,
        out_specs=(P(("groups", "space"), None),) * 4,
        check_vma=False,
    )
```

time: 293 us -> 71.5 us (0.24)
  waiting for transfers between devices: 183 us -> 0 us
  Pallas kernels: 0 us -> 58.1 us
  other arithmetic: 27.5 us -> 2.18 us
  matrix products: 20.5 us -> 0 us
  local copies, waits for them, and re-layouts: 30.6 us -> 10.1 us
  starting transfers between devices: 16.4 us -> 0 us
  between operations: 14 us -> 0.7 us
    reduce_scatter x2 -> x0, waiting for transfers between devices: 93.5 us -> none  [the longest x1 61.7 us: on_device(): lax.psum_scatter(factor * product, 'space', scatter_dimension=0, tiled=True)]
    unnamed x4 -> x0, waiting for transfers between devices: 61.1 us -> none
    pallas_call x0 -> x1, Pallas kernels: none -> 58.1 us  [on_device(): pl.pallas_call(functools.partial(kernel, (n, half, mols, reach, factor, f...]
    ppermute x4 -> x0, waiting for transfers between devices: 28.8 us -> none  [the longest x1 26.3 us: extended_2(): lax.ppermute(tail, axis, [(i, (i + 1) % count) for i in range(count)])]
    scatter-add x4 -> x0, other arithmetic: 26.9 us -> none  [the longest x1 13.7 us: on_device(): src_sum = jax.ops.segment_sum(grad_wide, edge_src, num_segments=mols)]
    dot_general x8 -> x0, matrix products: 20.5 us -> none  [the longest x1 7.8 us: on_device(): lax.dot_general(hidden, blocks, (((0,), (0,)), ((), ())), preferred_eleme...]
    gather x2 -> x0, local copies, waits for them, and re-layouts: 17.9 us -> none  [on_device(): pre = proj_src[edge_src] + proj_dst[edge_dst]]
    ppermute x4 -> x0, starting transfers between devices: 8.91 us -> none  [the longest x2 4.52 us: passed_along(): return lax.ppermute(block, axis, route)]
  transfers between devices with their start and end apart: 8 -> 0, of which waited for: 6 -> 0; matrix products, arithmetic and copies ran while one was open for 17% -> 0% of each run, Pallas kernels for 0% -> 0%
where the time goes in v1:
time: 71.5 us; the launch traced here: 71 us
  Pallas kernels  58.1 us (81%)
  local copies, waits for them, and re-layouts  10.1 us (14%)
  other arithmetic  2.18 us (3%)
    pallas_call x1, Pallas kernels, on_device(): pl.pallas_call(functools.partial(kernel, (n, half, mols, reach, factor, f...  58.1 us
    unnamed x12, local copies, waits for them, and re-layouts  9.98 us

profile of v1, /device:TPU:0, one launch (start us, length us, event | category | flops | bytes accessed | tf_op | source)
XLA Modules:
  0.0 71.0 jit_solution(11295920684969043085)
XLA Ops:
  0.6 0.7 compare_bitcast_fusion
  1.4 0.7 fusion.1
  2.1 0.7 add_select_fusion
  2.8 0.1 slice_select_fusion
  2.8 0.1 reshape.26
  2.9 1.4 %copy.15.w_out = bf16[512,529]{1,0:T(8,128)(2,1)S(1)} copy(bf16[512,529]{0,1:T(8,128)(2,1)} %param.11) | data formatting | bytes 1083392 | tf_op args[3]
  4.3 0.0 copy-start.2
  4.3 3.9 %copy.16.blocks = bf16[1,16,128,529]{3,2,1,0:T(8,128)(2,1)S(1)} copy(bf16[1,16,128,529]{2,1,3,0:T(8,128)(2,1)} %param.12) | data formatting | bytes 4333568 | tf_op args[4]
  8.2 0.0 copy-done.2
  8.2 0.0 copy-start
  8.2 1.0 %copy-done = bf16[512,512]{1,0:T(8,128)(2,1)S(1)} copy-done((bf16[512,512]{1,0:T(8,128)(2,1)S(1)}, bf16[512,512]{1,0:T(8,128)(2,1)}, u32[]{:S(2)}) %copy-start) | copy-done | bytes 524312
  9.2 0.0 copy-start.1
  9.2 1.0 %copy-done.1 = bf16[512,512]{1,0:T(8,128)(2,1)S(1)} copy-done((bf16[512,512]{1,0:T(8,128)(2,1)S(1)}, bf16[512,512]{1,0:T(8,128)(2,1)}, u32[]{:S(2)}) %copy-start.1) | copy-done | bytes 524312
  10.3 58.1 %shard_map.111 = (f32[256,512]{1,0:T(8,128)S(1)}, f32[32,512]{1,0:T(8,128)S(1)}, f32[32,512]{1,0:T(8,128)S(1)}, f32[32,529]{1,0:T(8,128)S(1)}) custom-call(bf16[256,512]{1,0:T(8,128)(2,1)S(1)} %copy-done.2, bf16[512,512]{1,0:T(8,128)(2,1)S(1)} %copy-done, bf16[512,512]{1,0:T(8,128)(2,1)S(1)} %copy-done.1, bf16[512,529]{1,0:T(8,128)(2,1)S(1)} %copy.15.w_out, ...), custom_call_target="tpu_custom_call" | custom-call | tf_op jit(solution)/shard_map/pallas_call | solution.py:312
  68.3 0.8 %copy.23 = f32[256,512]{1,0:T(8,128)} copy(f32[256,512]{1,0:T(8,128)S(1)} %get-tuple-element.8) | data formatting | bytes 1048576
  69.1 0.6 copy.24
  69.8 0.6 copy.25
  70.4 0.6 copy.26
  (3 shorter events, 0.0 us)
Async XLA Ops:
  4.3 3.9 %copy-start.2 = (bf16[256,512]{1,0:T(8,128)(2,1)S(1)}, bf16[256,512]{1,0:T(8,128)(2,1)}, u32[]{:S(2)}) copy-start(bf16[256,512]{1,0:T(8,128)(2,1)} %feats.1) | copy-start | bytes 786436
  8.2 1.0 %copy-start = (bf16[512,512]{1,0:T(8,128)(2,1)S(1)}, bf16[512,512]{1,0:T(8,128)(2,1)}, u32[]{:S(2)}) copy-start(bf16[512,512]{1,0:T(8,128)(2,1)} %w_src.1) | copy-start | bytes 1572868
  9.2 1.0 %copy-start.1 = (bf16[512,512]{1,0:T(8,128)(2,1)S(1)}, bf16[512,512]{1,0:T(8,128)(2,1)}, u32[]{:S(2)}) copy-start(bf16[512,512]{1,0:T(8,128)(2,1)} %w_dst.1) | copy-start | bytes 1572868

commit v2 on v1

--- a/solution.py
+++ b/solution.py
@@ -27,11 +27,12 @@
 
 
 def kernel(
-    dims, feats, w_src, w_dst, w_out, idx, idx_own, blocks, fgrad, src_out, dst_out, out_out,
-    halo, ext, own, recv, pt_hi, pt_lo, ft, oh, hid, fac, oh_own, hid_own, fac_own, sums, out_sum, back,
-    block_send, block_recv, halo_send, halo_recv, back_send, back_recv, own_sem, *rs,
+    dims, feats_far, w_src_far, w_dst_far, w_out_t, idx, idx_own, own, blocks, tails, fgrad, src_out, dst_out, out_out,
+    feats, w_src, w_dst, w_main, w_tail, halo, ext, recv, recv_tail, pt_hi, pt_lo, ft, oh, hid, fac, oh_own, hid_own,
+    fac_own, sums, out_sum, back, block_send, block_recv, tail_send, tail_recv, halo_send, halo_recv, back_send,
+    back_recv, load_sem, *rs,
 ):
-    n, half, mols, reach, factor, fused = dims
+    n, half, mols, reach, factor, fused, pack, base = dims
     quarter = n // 4
     chunk = quarter * half
     me = lax.axis_index("space")
@@ -44,8 +45,12 @@
     def _(k):
         pl.semaphore_signal(barrier, inc=1, device_id={"space": lax.rem(me + k, n)}, device_id_type=MESH)
 
-    local = pltpu.make_async_copy(blocks.at[0, me], own, own_sem)
-    local.start()
+    loads = [
+        pltpu.make_async_copy(far, near, load_sem.at[i])
+        for i, (far, near) in enumerate(((feats_far, feats), (w_src_far, w_src), (w_dst_far, w_dst)))
+    ]
+    for load in loads:
+        load.start()
     pl.semaphore_wait(barrier, n - 1)
 
     def remote(src, dst, send, arrive, device):
@@ -56,20 +61,34 @@
 
     def block_copy(source_slot, target):
         return remote(
-            blocks.at[0, target, pl.ds(0, half)], recv.at[source_slot],
-            block_send.at[target], block_recv.at[source_slot], target,
+            blocks.at[target], recv.at[source_slot], block_send.at[target], block_recv.at[source_slot], target
         )
 
-    up = remote(feats.at[pl.ds(mols - reach, reach)], halo.at[0], halo_send.at[0], halo_recv.at[0], above)
-    down = remote(feats.at[pl.ds(0, reach)], halo.at[1], halo_send.at[1], halo_recv.at[1], below)
+    def tail_copy(source_slot, target):
+        return remote(
+            tails.at[target], recv_tail.at[source_slot], tail_send.at[target], tail_recv.at[source_slot], target
+        )
+
+    up = remote(feats_far.at[pl.ds(mols - reach, reach)], halo.at[0], halo_send.at[0], halo_recv.at[0], above)
+    down = remote(feats_far.at[pl.ds(0, reach)], halo.at[1], halo_send.at[1], halo_recv.at[1], below)
     up.start()
     down.start()
 
     @pl.loop(1, n)
     def _(k):
         block_copy(me, lax.rem(me + k, n)).start()
+        tail_copy(me, lax.rem(me + k, n)).start()
 
     recv[me] = jnp.zeros(recv.shape[1:], BF16)
+    recv_tail[me] = jnp.zeros(recv_tail.shape[1:], BF16)
+    width = w_main.shape[0]
+    rest = w_out_t.shape[0] - width
+    w_main[...] = w_out_t[0:width].astype(F32).T.astype(BF16)
+    last = w_out_t[width:].astype(F32)
+    last = jnp.concatenate([last, jnp.zeros((w_tail.shape[1] - rest, width), F32)], axis=0)
+    w_tail[...] = last.T.astype(BF16)
+    for load in loads:
+        load.wait()
     ext[0:mols] = feats[...]
     pt = mm(feats[...], w_src[...]).T
     high, low = split(pt)
@@ -89,22 +108,23 @@
         return (lax.broadcasted_iota(jnp.int32, (count, ids.shape[1]), 0) == ids).astype(F32).astype(BF16)
 
     def ahead(ids, oh_ref, hid_ref, fac_ref):
-        oh_ref[0:mols] = one_hot(ids[0:1], mols)
-        oh_ref[mols:] = one_hot(ids[1:2], mols + 2 * reach)
+        oh_ref[0:mols] = one_hot(lax.shift_right_arithmetic(ids, base), mols)
+        oh_ref[mols:] = one_hot(ids & ((1 << base) - 1), mols + 2 * reach)
         pre = mm(pt_hi[...], oh_ref[...]) + mm(pt_lo[...], oh_ref[...])
         sigma = jax.nn.sigmoid(pre)
         hid_ref[...] = (pre * sigma).astype(BF16)
         fac_ref[...] = sigma * (1.0 + pre * (1.0 - sigma))
 
-    def terms(g, oh_ref, hid_ref, fac_ref):
-        dpre = (mm_nt(w_out[...], g) * fac_ref[...]).astype(BF16)
-        return mm_nt(oh_ref[...], dpre), mm(hid_ref[...], g)
+    def terms(g, tail, oh_ref, hid_ref, fac_ref):
+        dhidden = mm_nt(w_main[...], g) + mm_nt(w_tail[...], tail)
+        dpre = (dhidden * fac_ref[...]).astype(BF16)
+        return mm_nt(oh_ref[...], dpre), mm(hid_ref[...], g), mm(hid_ref[...], tail)[:, 0:rest]
 
     ahead(idx_own[...], oh_own, hid_own, fac_own)
-    local.wait()
-    s, o = terms(own[...], oh_own, hid_own, fac_own)
+    s, o, t = terms(own[:, 0:width], own[:, width:], oh_own, hid_own, fac_own)
     sums[...] = s
-    out_sum[...] = o
+    out_sum[:, 0:width] = o
+    out_sum[:, width:] = t
 
     @pl.loop(0, 4)
     def _(c):
@@ -120,12 +140,18 @@
 
             @pl.when(owner != me)
             def _():
-                block_copy(owner, lax.rem(owner + 0, n)).wait_recv()
-
-        g = recv[pl.ds(c * quarter, quarter)].reshape(chunk, recv.shape[2])
-        s, o = terms(g, oh.at[c], hid.at[c], fac.at[c])
+                block_copy(owner, owner).wait_recv()
+                tail_copy(owner, owner).wait_recv()
+
+        g = recv[pl.ds(c * quarter, quarter)].reshape(quarter, pack, half // pack, width)
+        g = jnp.concatenate([g[:, p].reshape(chunk // pack, width) for p in range(pack)], axis=0)
+        tail = recv_tail[pl.ds(c * quarter, quarter)].reshape(chunk // pack, recv_tail.shape[2]).astype(F32)
+        span = w_tail.shape[1]
+        tail = jnp.concatenate([tail[:, p * span : (p + 1) * span] for p in range(pack)], axis=0).astype(BF16)
+        s, o, t = terms(g, tail, oh.at[c], hid.at[c], fac.at[c])
         sums[...] += s
-        out_sum[...] += o
+        out_sum[:, 0:width] += o
+        out_sum[:, width:] += t
 
     give_down = remote(sums.at[pl.ds(2 * mols, reach)], back.at[1], back_send.at[0], back_recv.at[1], below)
     give_up = remote(sums.at[pl.ds(2 * mols + reach, reach)], back.at[0], back_send.at[1], back_recv.at[0], above)
@@ -245,6 +271,7 @@
     @pl.loop(1, n)
     def _(k):
         block_copy(me, lax.rem(me + k, n)).wait_send()
+        tail_copy(me, lax.rem(me + k, n)).wait_send()
 
 
 def on_device(mol_feats, w_src, w_dst, w_out, grad_blocks, edge_src, edge_dst, edge_live):
@@ -264,21 +291,36 @@
     below = edge_dst < reach
     inside = edge_dst < reach + mols
     target = jnp.where(below, edge_dst + mols, jnp.where(inside, edge_dst - reach, edge_dst))
-    ids = jnp.stack([edge_src, target]).reshape(2, n, cap)
-    ids = jnp.where(edge_live.reshape(1, n, cap) > 0, ids, -1)
-    idx_own = lax.dynamic_index_in_dim(ids, me, 1, keepdims=False)
-    own_row = lax.broadcasted_iota(jnp.int32, (2, n, half), 1) == me
-    idx = jnp.where(own_row, -1, ids[:, :, :half]).reshape(2, 4, chunk).transpose(1, 0, 2)
+    base = (mols + 2 * reach).bit_length()
+    ids = jnp.where(edge_live > 0, (edge_src << base) + target, -1).reshape(n, cap)
+    pack = 4 if half % 64 == 0 else 1
+    tail_span = 128 // pack
+    idx_own = lax.dynamic_slice_in_dim(ids, me, 1, axis=0)
+    own_row = lax.broadcasted_iota(jnp.int32, (n, half), 0) == me
+    idx = jnp.where(own_row, -1, ids[:, :half]).reshape(4, quarter, pack, half // pack)
+    idx = idx.transpose(0, 2, 1, 3).reshape(4, 1, chunk)
+    first = grad_blocks[0, :, :half]
+    blocks = first[:, :, :width]
+    rest = entries - width
+    tails = jnp.pad(first[:, :, width:], ((0, 0), (0, 0), (0, tail_span - rest)))
+    tails = tails.reshape(n, pack, half // pack, tail_span).transpose(0, 2, 1, 3).reshape(n, half // pack, 128)
+    own = lax.dynamic_index_in_dim(grad_blocks[0], me, 0, keepdims=False)
+    own = jnp.pad(own, ((0, 0), (0, tail_span - rest)))
 
     span = mols + 2 * reach
     count = mols + span
     vm = pltpu.VMEM
     dma = pltpu.SemaphoreType.DMA
     scratch = [
+        vm((mols, width), BF16),
+        vm((width, width), BF16),
+        vm((width, width), BF16),
+        vm((width, width), BF16),
+        vm((width, tail_span), BF16),
         vm((2, reach, width), BF16),
         vm((span, width), BF16),
-        vm((cap, entries), BF16),
-        vm((n, half, entries), BF16),
+        vm((n, half, width), BF16),
+        vm((n, half // pack, 128), BF16),
         vm((width, count), BF16),
         vm((width, count), BF16),
         vm((width, span), BF16),
@@ -291,7 +333,7 @@
         vm((count, width), F32),
         vm((width, entries), F32),
         vm((2, reach, width), F32),
-        dma((n,)), dma((n,)), dma((2,)), dma((2,)), dma((2,)), dma((2,)), dma(()),
+        dma((n,)), dma((n,)), dma((n,)), dma((n,)), dma((2,)), dma((2,)), dma((2,)), dma((2,)), dma((3,)),
     ]
     if fused:
         for columns in (entries, width, width):
@@ -309,21 +351,23 @@
         scratch += [dma((3,)), dma((3,)), dma((3,)), dma((3,)), dma((3, quarter)), dma((3, quarter))]
     out_rows = rows if fused else width
     whole = pl.BlockSpec(memory_space=pltpu.VMEM)
+    near = pl.BlockSpec(memory_space=pl.ANY)
+    far = pl.BlockSpec(memory_space=pltpu.HBM)
     fgrad, src_g, dst_g, out_g = pl.pallas_call(
-        functools.partial(kernel, (n, half, mols, reach, factor, fused)),
+        functools.partial(kernel, (n, half, mols, reach, factor, fused, pack, base)),
         out_shape=(
             jax.ShapeDtypeStruct((mols, width), F32),
             jax.ShapeDtypeStruct((out_rows, width), F32),
             jax.ShapeDtypeStruct((out_rows, width), F32),
             jax.ShapeDtypeStruct((out_rows, entries), F32),
         ),
-        in_specs=[whole] * 6 + [pl.BlockSpec(memory_space=pl.ANY)],
+        in_specs=[far] * 3 + [whole] * 4 + [near] * 2,
         out_specs=(whole,) * 4,
         scratch_shapes=scratch,
         compiler_params=pltpu.CompilerParams(
             collective_id=0, has_side_effects=True, vmem_limit_bytes=48 * 1024 * 1024
         ),
-    )(mol_feats, w_src, w_dst, w_out, idx, idx_own, grad_blocks)
+    )(mol_feats, w_src, w_dst, w_out.T, idx, idx_own, own, blocks, tails)
     if not fused:
         src_g, dst_g, out_g = [
             lax.psum_scatter(part, "space", scatter_dimension=0, tiled=True) for part in (src_g, dst_g, out_g)

time: 71.5 us -> 67.5 us (0.944)
  Pallas kernels: 58.1 us -> 54.4 us
  other arithmetic: 2.18 us -> 0.82 us
  local copies, waits for them, and re-layouts: 10.1 us -> 11.1 us
    pallas_call x1, Pallas kernels: 58.1 us -> 54.4 us  [on_device(): pl.pallas_call(functools.partial(kernel, (n, half, mols, reach, factor, f...]
    unnamed x12 -> x15, local copies, waits for them, and re-layouts: 9.98 us -> 7.52 us
    dynamic_slice x1 -> x3, local copies, waits for them, and re-layouts: 0.01 us -> 1.71 us  [the longest x2 1.7 us: on_device(): own = lax.dynamic_index_in_dim(grad_blocks[0], me, 0, keepdims=False)]
    slice x0 -> x2, local copies, waits for them, and re-layouts: none -> 1.36 us  [the longest x1 1.32 us: on_device(): blocks = first[:, :, :width]]
    reshape x0 -> x1, other arithmetic: none -> 0.74 us  [on_device(): jnp.where(edge_live > 0, (edge_src << base) + target, -1).reshape(n, cap)]
where the time goes in v2:
time: 67.5 us; the launch traced here: 67.2 us
  Pallas kernels  54.4 us (81%)
  local copies, waits for them, and re-layouts  11.1 us (16%)
  other arithmetic  0.82 us (1%)
  between operations  0.79 us (1%)
    pallas_call x1, Pallas kernels, on_device(): pl.pallas_call(functools.partial(kernel, (n, half, mols, reach, factor, f...  54.4 us
    unnamed x15, local copies, waits for them, and re-layouts  7.52 us
    dynamic_slice x2, local copies, waits for them, and re-layouts, on_device(): own = lax.dynamic_index_in_dim(grad_blocks[0], me, 0, keepdims=False)  1.7 us

profile of v2, /device:TPU:0, one launch (start us, length us, event | category | flops | bytes accessed | tf_op | source)
XLA Modules:
  0.0 67.2 jit_solution(7027263624013270730)
XLA Ops:
  0.6 0.7 %fusion.3 = s32[16,128]{1,0:T(8,128)S(1)} fusion(s32[2048]{0:T(1024)} %param.14, s32[2048]{0:T(1024)} %param.13, s32[2048]{0:T(1024)} %param.15), kind=kLoop, calls=%fused_computation.5 | loop fusion | flops 20480 | bytes 32768 | tf_op jit(solution)/shard_map/reshape | solution.py:295
  1.4 0.1 slice_select_fusion
  1.5 0.1 reshape.26
  1.6 0.1 reshape.27.idx
  1.7 1.5 %constant_dynamic-slice_fusion = bf16[1,1,128,529]{2,1,3,0:T(2,128)(2,1)S(1)} fusion(bf16[1,16,128,529]{2,1,3,0:T(8,128)(2,1)} %param.12, s32[]{:T(128)S(6)} %select_n.24), kind=kLoop, calls=%fused_computation.7 | loop fusion | bytes 270852 | tf_op jit(solution)/shard_map/jit(dynamic_index_in_dim)/dynamic_slice | solution.py:307
  3.2 0.2 copy.13
  3.4 3.8 %copy.16 = bf16[1,16,64,529]{3,2,1,0:T(8,128)(2,1)S(1)} copy(bf16[1,16,64,529]{2,1,3,0:T(8,128)(2,1)} %bitcast.14) | data formatting | bytes 2166784
  7.2 0.0 copy-start.4
  7.2 0.0 copy-start
  7.2 0.0 copy-start.1
  7.2 0.0 copy-start.2
  7.3 0.0 copy-start.3
  7.3 1.0 %copy-done.4 = bf16[1,16,64,529]{3,2,1,0:T(8,128)(2,1)} copy-done((bf16[1,16,64,529]{3,2,1,0:T(8,128)(2,1)}, bf16[1,16,64,529]{3,2,1,0:T(8,128)(2,1)S(1)}, u32[]{:S(2)}) %copy-start.4) | copy-done | bytes 1083416
  8.3 1.3 %slice.17.blocks = bf16[16,64,512]{2,1,0:T(8,128)(2,1)S(1)} slice(bf16[16,64,529]{2,1,0:T(8,128)(2,1)} %bitcast.13), slice={[0:16], [0:64], [0:512]} | slice | bytes 2097152 | tf_op jit(solution)/shard_map/slice | solution.py:303
  9.6 0.1 pad.9
  9.7 0.1 copy.18
  9.8 0.2 reshape.29.tails
  10.0 0.0 copy-done
  10.0 0.0 copy-done.1
  10.0 0.0 copy-done.2
  10.0 0.0 copy-done.3
  10.1 54.4 %shard_map.111 = (f32[256,512]{1,0:T(8,128)S(1)}, f32[32,512]{1,0:T(8,128)S(1)}, f32[32,512]{1,0:T(8,128)S(1)}, f32[32,529]{1,0:T(8,128)S(1)}) custom-call(bf16[256,512]{1,0:T(8,128)(2,1)S(1)} %copy-done.3, bf16[512,512]{1,0:T(8,128)(2,1)S(1)} %copy-done.1, bf16[512,512]{1,0:T(8,128)(2,1)S(1)} %copy-done.2, bf16[529,512]{1,0:T(8,128)(2,1)S(1)} %bitcast.11, ...), custom_call_target="tpu_custom_call" | custom-call | tf_op jit(solution)/shard_map/pallas_call | solution.py:356
  64.5 0.8 %copy.23 = f32[256,512]{1,0:T(8,128)} copy(f32[256,512]{1,0:T(8,128)S(1)} %get-tuple-element.8) | data formatting | bytes 1048576
  65.3 0.6 copy.24
  65.9 0.6 copy.25
  66.5 0.6 copy.26
  (5 shorter events, 0.1 us)
Async XLA Ops:
  7.2 1.1 %copy-start.4 = (bf16[1,16,64,529]{3,2,1,0:T(8,128)(2,1)}, bf16[1,16,64,529]{3,2,1,0:T(8,128)(2,1)S(1)}, u32[]{:S(2)}) copy-start(bf16[1,16,64,529]{3,2,1,0:T(8,128)(2,1)S(1)} %copy.16) | copy-start | bytes 3250180
  7.2 2.8 %copy-start = (bf16[512,529]{0,1:T(8,128)(2,1)S(1)}, bf16[512,529]{0,1:T(8,128)(2,1)}, u32[]{:S(2)}) copy-start(bf16[512,529]{0,1:T(8,128)(2,1)} %param.11) | copy-start | bytes 1625092
  7.2 2.8 %copy-start.1 = (bf16[512,512]{1,0:T(8,128)(2,1)S(1)}, bf16[512,512]{1,0:T(8,128)(2,1)}, u32[]{:S(2)}) copy-start(bf16[512,512]{1,0:T(8,128)(2,1)} %w_src_far.1) | copy-start | bytes 1572868
  7.2 2.8 %copy-start.2 = (bf16[512,512]{1,0:T(8,128)(2,1)S(1)}, bf16[512,512]{1,0:T(8,128)(2,1)}, u32[]{:S(2)}) copy-start(bf16[512,512]{1,0:T(8,128)(2,1)} %w_dst_far.1) | copy-start | bytes 1572868
  7.3 2.8 %copy-start.3 = (bf16[256,512]{1,0:T(8,128)(2,1)S(1)}, bf16[256,512]{1,0:T(8,128)(2,1)}, u32[]{:S(2)}) copy-start(bf16[256,512]{1,0:T(8,128)(2,1)} %feats_far.1) | copy-start | bytes 786436

commit v3 on v2

--- a/solution.py
+++ b/solution.py
@@ -27,14 +27,15 @@
 
 
 def kernel(
-    dims, feats_far, w_src_far, w_dst_far, w_out_t, idx, idx_own, own, blocks, tails, fgrad, src_out, dst_out, out_out,
-    feats, w_src, w_dst, w_main, w_tail, halo, ext, recv, recv_tail, pt_hi, pt_lo, ft, oh, hid, fac, oh_own, hid_own,
+    dims, feats_far, w_src_far, w_dst_far, w_out_t, idx, idx_own, blocks, tails, fgrad, src_out, dst_out, out_out,
+    own, feats, w_src, w_dst, w_main, w_tail, halo, ext, recv, recv_tail, pt_hi, pt_lo, ft, oh, hid, fac, oh_own, hid_own,
     fac_own, sums, out_sum, back, block_send, block_recv, tail_send, tail_recv, halo_send, halo_recv, back_send,
     back_recv, load_sem, *rs,
 ):
     n, half, mols, reach, factor, fused, pack, base = dims
     quarter = n // 4
     chunk = quarter * half
+    width = w_main.shape[0]
     me = lax.axis_index("space")
     above = lax.rem(me + 1, n)
     below = lax.rem(me + n - 1, n)
@@ -45,10 +46,8 @@
     def _(k):
         pl.semaphore_signal(barrier, inc=1, device_id={"space": lax.rem(me + k, n)}, device_id_type=MESH)
 
-    loads = [
-        pltpu.make_async_copy(far, near, load_sem.at[i])
-        for i, (far, near) in enumerate(((feats_far, feats), (w_src_far, w_src), (w_dst_far, w_dst)))
-    ]
+    pairs = ((feats_far, feats), (w_src_far, w_src), (w_dst_far, w_dst), (blocks.at[me], own))
+    loads = [pltpu.make_async_copy(far, near, load_sem.at[i]) for i, (far, near) in enumerate(pairs)]
     for load in loads:
         load.start()
     pl.semaphore_wait(barrier, n - 1)
@@ -61,7 +60,8 @@
 
     def block_copy(source_slot, target):
         return remote(
-            blocks.at[target], recv.at[source_slot], block_send.at[target], block_recv.at[source_slot], target
+            blocks.at[target, pl.ds(0, half), pl.ds(0, width)], recv.at[source_slot],
+            block_send.at[target], block_recv.at[source_slot], target,
         )
 
     def tail_copy(source_slot, target):
@@ -76,12 +76,12 @@
 
     @pl.loop(1, n)
     def _(k):
-        block_copy(me, lax.rem(me + k, n)).start()
-        tail_copy(me, lax.rem(me + k, n)).start()
+        target = lax.rem(me + 7 * k, n)
+        block_copy(me, target).start()
+        tail_copy(me, target).start()
 
     recv[me] = jnp.zeros(recv.shape[1:], BF16)
     recv_tail[me] = jnp.zeros(recv_tail.shape[1:], BF16)
-    width = w_main.shape[0]
     rest = w_out_t.shape[0] - width
     w_main[...] = w_out_t[0:width].astype(F32).T.astype(BF16)
     last = w_out_t[width:].astype(F32)
@@ -120,8 +120,11 @@
         dpre = (dhidden * fac_ref[...]).astype(BF16)
         return mm_nt(oh_ref[...], dpre), mm(hid_ref[...], g), mm(hid_ref[...], tail)[:, 0:rest]
 
+    own_tail = jnp.concatenate(
+        [own[:, width:].astype(F32), jnp.zeros((own.shape[0], w_tail.shape[1] - rest), F32)], axis=1
+    ).astype(BF16)
     ahead(idx_own[...], oh_own, hid_own, fac_own)
-    s, o, t = terms(own[:, 0:width], own[:, width:], oh_own, hid_own, fac_own)
+    s, o, t = terms(own[:, 0:width], own_tail, oh_own, hid_own, fac_own)
     sums[...] = s
     out_sum[:, 0:width] = o
     out_sum[:, width:] = t
@@ -274,6 +277,14 @@
         tail_copy(me, lax.rem(me + k, n)).wait_send()
 
 
+def write_out(*refs):
+    copies = [pltpu.make_async_copy(refs[i], refs[4 + i], refs[8].at[i]) for i in range(4)]
+    for copy in copies:
+        copy.start()
+    for copy in copies:
+        copy.wait()
+
+
 def on_device(mol_feats, w_src, w_dst, w_out, grad_blocks, edge_src, edge_dst, edge_live):
     mols, width = mol_feats.shape
     entries = w_out.shape[1]
@@ -299,19 +310,17 @@
     own_row = lax.broadcasted_iota(jnp.int32, (n, half), 0) == me
     idx = jnp.where(own_row, -1, ids[:, :half]).reshape(4, quarter, pack, half // pack)
     idx = idx.transpose(0, 2, 1, 3).reshape(4, 1, chunk)
-    first = grad_blocks[0, :, :half]
-    blocks = first[:, :, :width]
+    blocks = grad_blocks[0]
     rest = entries - width
-    tails = jnp.pad(first[:, :, width:], ((0, 0), (0, 0), (0, tail_span - rest)))
+    tails = jnp.pad(blocks[:, :half, width:], ((0, 0), (0, 0), (0, tail_span - rest)))
     tails = tails.reshape(n, pack, half // pack, tail_span).transpose(0, 2, 1, 3).reshape(n, half // pack, 128)
-    own = lax.dynamic_index_in_dim(grad_blocks[0], me, 0, keepdims=False)
-    own = jnp.pad(own, ((0, 0), (0, tail_span - rest)))
 
     span = mols + 2 * reach
     count = mols + span
     vm = pltpu.VMEM
     dma = pltpu.SemaphoreType.DMA
     scratch = [
+        vm((cap, entries), BF16),
         vm((mols, width), BF16),
         vm((width, width), BF16),
         vm((width, width), BF16),
@@ -333,7 +342,7 @@
         vm((count, width), F32),
         vm((width, entries), F32),
         vm((2, reach, width), F32),
-        dma((n,)), dma((n,)), dma((n,)), dma((n,)), dma((2,)), dma((2,)), dma((2,)), dma((2,)), dma((3,)),
+        dma((n,)), dma((n,)), dma((n,)), dma((n,)), dma((2,)), dma((2,)), dma((2,)), dma((2,)), dma((4,)),
     ]
     if fused:
         for columns in (entries, width, width):
@@ -361,18 +370,26 @@
             jax.ShapeDtypeStruct((out_rows, width), F32),
             jax.ShapeDtypeStruct((out_rows, entries), F32),
         ),
-        in_specs=[far] * 3 + [whole] * 4 + [near] * 2,
+        in_specs=[far] * 3 + [whole] * 3 + [near] * 2,
         out_specs=(whole,) * 4,
         scratch_shapes=scratch,
         compiler_params=pltpu.CompilerParams(
             collective_id=0, has_side_effects=True, vmem_limit_bytes=48 * 1024 * 1024
         ),
-    )(mol_feats, w_src, w_dst, w_out.T, idx, idx_own, own, blocks, tails)
+    )(mol_feats, w_src, w_dst, w_out.T, idx, idx_own, blocks, tails)
     if not fused:
         src_g, dst_g, out_g = [
             lax.psum_scatter(part, "space", scatter_dimension=0, tiled=True) for part in (src_g, dst_g, out_g)
         ]
-    return fgrad, src_g, dst_g, out_g
+        return fgrad, src_g, dst_g, out_g
+    results = (fgrad, src_g, dst_g, out_g)
+    return pl.pallas_call(
+        write_out,
+        out_shape=tuple(jax.ShapeDtypeStruct(r.shape, r.dtype) for r in results),
+        in_specs=[near] * 4,
+        out_specs=(far,) * 4,
+        scratch_shapes=[dma((4,))],
+    )(*results)
 
 
 def solution(mesh):

time: 67.5 us -> 89.6 us (1.33)
  Pallas kernels: 54.4 us -> 76.8 us
    pallas_call x0 -> x1, Pallas kernels: none -> 23.5 us  [on_device(): pl.pallas_call(write_out, out_shape=tuple((jax.ShapeDtypeStruct(r.shape,...]
    dynamic_slice x2 -> x0, local copies, waits for them, and re-layouts: 1.7 us -> none  [on_device(): own = lax.dynamic_index_in_dim(grad_blocks[0], me, 0, keepdims=False)]
    reshape x2, local copies, waits for them, and re-layouts: 0.28 us -> 1.98 us  [on_device(): tails.reshape(n, pack, half // pack, tail_span).transpose(0, 2, 1, 3)]
    slice x2 -> x1, local copies, waits for them, and re-layouts: 1.36 us -> 0.05 us  [on_device(): blocks[:, :half, width:]]
    unnamed x15 -> x17, local copies, waits for them, and re-layouts: 7.52 us -> 8.63 us
    pallas_call x1, Pallas kernels: 54.4 us -> 53.4 us  [on_device(): pl.pallas_call(functools.partial(kernel, (n, half, mols, reach, factor, f...]
where the time goes in v3:
time: 89.6 us; the launch traced here: 89.3 us
  Pallas kernels  76.8 us (86%)
  local copies, waits for them, and re-layouts  10.9 us (12%)
    pallas_call x1, Pallas kernels, on_device(): pl.pallas_call(functools.partial(kernel, (n, half, mols, reach, factor, f...  53.4 us
    pallas_call x1, Pallas kernels, on_device(): pl.pallas_call(write_out, out_shape=tuple((jax.ShapeDtypeStruct(r.shape,...  23.5 us
    unnamed x17, local copies, waits for them, and re-layouts  8.63 us
    reshape x2, local copies, waits for them, and re-layouts, on_device(): tails.reshape(n, pack, half // pack, tail_span).transpose(0, 2, 1, 3)  1.98 us

profile of v3, /device:TPU:0, one launch (start us, length us, event | category | flops | bytes accessed | tf_op | source)
XLA Modules:
  0.0 89.3 jit_solution(9252390152745500699)
XLA Ops:
  0.6 0.7 fusion.3
  1.4 0.1 slice_select_fusion
  1.5 0.1 reshape.24
  1.6 0.1 reshape.25.idx
  1.7 0.0 copy-start
  1.7 0.0 copy-start.4
  1.7 3.9 %copy.13 = bf16[1,16,128,529]{3,2,1,0:T(8,128)(2,1)S(1)} copy(bf16[1,16,128,529]{2,1,3,0:T(8,128)(2,1)} %param.12) | data formatting | bytes 4333568 | tf_op args[4]
  5.6 0.1 pad.4
  5.7 0.8 copy.16
  6.5 1.2 %reshape.27.tails = bf16[16,16,128]{2,1,0:T(8,128)(2,1)S(1)} reshape(bf16[16,16,4,32]{3,2,1,0:T(4,128)(2,1)} %bitcast.13) | data formatting | bytes 131072 | tf_op jit(solution)/shard_map/reshape | solution.py:316
  7.7 0.0 copy-done
  7.7 0.0 copy-done.4
  7.7 0.0 copy-start.2
  7.7 1.0 %copy-done.2 = bf16[512,512]{1,0:T(8,128)(2,1)S(1)} copy-done((bf16[512,512]{1,0:T(8,128)(2,1)S(1)}, bf16[512,512]{1,0:T(8,128)(2,1)}, u32[]{:S(2)}) %copy-start.2) | copy-done | bytes 524312
  8.8 0.0 copy-start.3
  8.8 1.0 %copy-done.3 = bf16[512,512]{1,0:T(8,128)(2,1)S(1)} copy-done((bf16[512,512]{1,0:T(8,128)(2,1)S(1)}, bf16[512,512]{1,0:T(8,128)(2,1)}, u32[]{:S(2)}) %copy-start.3) | copy-done | bytes 524312
  9.8 53.4 %shard_map.111 = (f32[256,512]{1,0:T(8,128)S(1)}, f32[32,512]{1,0:T(8,128)S(1)}, f32[32,512]{1,0:T(8,128)S(1)}, f32[32,529]{1,0:T(8,128)S(1)}) custom-call(bf16[256,512]{1,0:T(8,128)(2,1)S(1)} %copy-done.4, bf16[512,512]{1,0:T(8,128)(2,1)S(1)} %copy-done.2, bf16[512,512]{1,0:T(8,128)(2,1)S(1)} %copy-done.3, bf16[529,512]{1,0:T(8,128)(2,1)S(1)} %bitcast.11, ...), custom_call_target="tpu_custom_call" | custom-call | tf_op jit(solution)/shard_map/pallas_call | solution.py:365
  63.2 0.0 copy-start.1
  63.2 0.8 copy-done.1
  64.0 0.0 copy-start.5
  64.0 0.6 copy-done.5
  64.6 0.0 copy-start.6
  64.6 0.6 copy-done.6
  65.2 0.0 copy-start.7
  65.2 0.6 copy-done.7
  65.8 23.5 %shard_map.112 = (f32[256,512]{1,0:T(8,128)}, f32[32,512]{1,0:T(8,128)}, f32[32,512]{1,0:T(8,128)}, f32[32,529]{1,0:T(8,128)}) custom-call(f32[256,512]{1,0:T(8,128)} %copy-done.1, f32[32,512]{1,0:T(8,128)} %copy-done.6, f32[32,512]{1,0:T(8,128)} %copy-done.7, f32[32,529]{1,0:T(8,128)} %copy-done.5), custom_call_target="tpu_custom_call" | custom-call | tf_op jit(solution)/shard_map/pallas_call | solution.py:386
  (4 shorter events, 0.1 us)
Async XLA Ops:
  1.7 6.0 %copy-start = (bf16[512,529]{0,1:T(8,128)(2,1)S(1)}, bf16[512,529]{0,1:T(8,128)(2,1)}, u32[]{:S(2)}) copy-start(bf16[512,529]{0,1:T(8,128)(2,1)} %param.11) | copy-start | bytes 1625092
  1.7 6.0 %copy-start.4 = (bf16[256,512]{1,0:T(8,128)(2,1)S(1)}, bf16[256,512]{1,0:T(8,128)(2,1)}, u32[]{:S(2)}) copy-start(bf16[256,512]{1,0:T(8,128)(2,1)} %feats_far.1) | copy-start | bytes 786436
  7.7 1.0 %copy-start.2 = (bf16[512,512]{1,0:T(8,128)(2,1)S(1)}, bf16[512,512]{1,0:T(8,128)(2,1)}, u32[]{:S(2)}) copy-start(bf16[512,512]{1,0:T(8,128)(2,1)} %w_src_far.1) | copy-start | bytes 1572868
  8.8 1.0 %copy-start.3 = (bf16[512,512]{1,0:T(8,128)(2,1)S(1)}, bf16[512,512]{1,0:T(8,128)(2,1)}, u32[]{:S(2)}) copy-start(bf16[512,512]{1,0:T(8,128)(2,1)} %w_dst_far.1) | copy-start | bytes 1572868
  63.2 0.8 copy-start.1
  64.0 0.6 copy-start.5
  64.6 0.6 copy-start.6
  65.2 0.6 copy-start.7

commit v4 on v3

--- a/solution.py
+++ b/solution.py
@@ -27,8 +27,8 @@
 
 
 def kernel(
-    dims, feats_far, w_src_far, w_dst_far, w_out_t, idx, idx_own, blocks, tails, fgrad, src_out, dst_out, out_out,
-    own, feats, w_src, w_dst, w_main, w_tail, halo, ext, recv, recv_tail, pt_hi, pt_lo, ft, oh, hid, fac, oh_own, hid_own,
+    dims, feats_far, w_src_far, w_dst_far, w_out_t, idx, idx_own, blocks, fgrad, src_out, dst_out, out_out,
+    own, mine, tails, feats, w_src, w_dst, w_main, w_tail, halo, ext, recv, recv_tail, pt_hi, pt_lo, ft, oh, hid, fac, oh_own, hid_own,
     fac_own, sums, out_sum, back, block_send, block_recv, tail_send, tail_recv, halo_send, halo_recv, back_send,
     back_recv, load_sem, *rs,
 ):
@@ -46,7 +46,7 @@
     def _(k):
         pl.semaphore_signal(barrier, inc=1, device_id={"space": lax.rem(me + k, n)}, device_id_type=MESH)
 
-    pairs = ((feats_far, feats), (w_src_far, w_src), (w_dst_far, w_dst), (blocks.at[me], own))
+    pairs = ((feats_far, feats), (w_src_far, w_src), (w_dst_far, w_dst), (blocks.at[me], own), (blocks.at[:, pl.ds(0, half)], mine))
     loads = [pltpu.make_async_copy(far, near, load_sem.at[i]) for i, (far, near) in enumerate(pairs)]
     for load in loads:
         load.start()
@@ -76,18 +76,28 @@
 
     @pl.loop(1, n)
     def _(k):
-        target = lax.rem(me + 7 * k, n)
-        block_copy(me, target).start()
+        block_copy(me, lax.rem(me + k, n)).start()
+
+    rest = w_out_t.shape[0] - width
+    span = w_tail.shape[1]
+    loads[4].wait()
+
+    @pl.loop(1, n)
+    def _(k):
+        target = lax.rem(me + k, n)
+        tail = mine[target, :, width:].astype(F32)
+        tail = jnp.concatenate([tail, jnp.zeros((half, span - rest), F32)], axis=1)
+        tail = tail.reshape(pack, half // pack, span)
+        tails[target] = jnp.concatenate([tail[p] for p in range(pack)], axis=1).astype(BF16)
         tail_copy(me, target).start()
 
     recv[me] = jnp.zeros(recv.shape[1:], BF16)
     recv_tail[me] = jnp.zeros(recv_tail.shape[1:], BF16)
-    rest = w_out_t.shape[0] - width
     w_main[...] = w_out_t[0:width].astype(F32).T.astype(BF16)
     last = w_out_t[width:].astype(F32)
     last = jnp.concatenate([last, jnp.zeros((w_tail.shape[1] - rest, width), F32)], axis=0)
     w_tail[...] = last.T.astype(BF16)
-    for load in loads:
+    for load in loads[0:4]:
         load.wait()
     ext[0:mols] = feats[...]
     pt = mm(feats[...], w_src[...]).T
@@ -149,7 +159,6 @@
         g = recv[pl.ds(c * quarter, quarter)].reshape(quarter, pack, half // pack, width)
         g = jnp.concatenate([g[:, p].reshape(chunk // pack, width) for p in range(pack)], axis=0)
         tail = recv_tail[pl.ds(c * quarter, quarter)].reshape(chunk // pack, recv_tail.shape[2]).astype(F32)
-        span = w_tail.shape[1]
         tail = jnp.concatenate([tail[:, p * span : (p + 1) * span] for p in range(pack)], axis=0).astype(BF16)
         s, o, t = terms(g, tail, oh.at[c], hid.at[c], fac.at[c])
         sums[...] += s
@@ -277,14 +286,6 @@
         tail_copy(me, lax.rem(me + k, n)).wait_send()
 
 
-def write_out(*refs):
-    copies = [pltpu.make_async_copy(refs[i], refs[4 + i], refs[8].at[i]) for i in range(4)]
-    for copy in copies:
-        copy.start()
-    for copy in copies:
-        copy.wait()
-
-
 def on_device(mol_feats, w_src, w_dst, w_out, grad_blocks, edge_src, edge_dst, edge_live):
     mols, width = mol_feats.shape
     entries = w_out.shape[1]
@@ -311,9 +312,6 @@
     idx = jnp.where(own_row, -1, ids[:, :half]).reshape(4, quarter, pack, half // pack)
     idx = idx.transpose(0, 2, 1, 3).reshape(4, 1, chunk)
     blocks = grad_blocks[0]
-    rest = entries - width
-    tails = jnp.pad(blocks[:, :half, width:], ((0, 0), (0, 0), (0, tail_span - rest)))
-    tails = tails.reshape(n, pack, half // pack, tail_span).transpose(0, 2, 1, 3).reshape(n, half // pack, 128)
 
     span = mols + 2 * reach
     count = mols + span
@@ -321,6 +319,8 @@
     dma = pltpu.SemaphoreType.DMA
     scratch = [
         vm((cap, entries), BF16),
+        vm((n, half, entries), BF16),
+        vm((n, half // pack, 128), BF16),
         vm((mols, width), BF16),
         vm((width, width), BF16),
         vm((width, width), BF16),
@@ -342,7 +342,7 @@
         vm((count, width), F32),
         vm((width, entries), F32),
         vm((2, reach, width), F32),
-        dma((n,)), dma((n,)), dma((n,)), dma((n,)), dma((2,)), dma((2,)), dma((2,)), dma((2,)), dma((4,)),
+        dma((n,)), dma((n,)), dma((n,)), dma((n,)), dma((2,)), dma((2,)), dma((2,)), dma((2,)), dma((5,)),
     ]
     if fused:
         for columns in (entries, width, width):
@@ -370,26 +370,18 @@
             jax.ShapeDtypeStruct((out_rows, width), F32),
             jax.ShapeDtypeStruct((out_rows, entries), F32),
         ),
-        in_specs=[far] * 3 + [whole] * 3 + [near] * 2,
+        in_specs=[far] * 3 + [whole] * 3 + [near],
         out_specs=(whole,) * 4,
         scratch_shapes=scratch,
         compiler_params=pltpu.CompilerParams(
-            collective_id=0, has_side_effects=True, vmem_limit_bytes=48 * 1024 * 1024
+            collective_id=0, has_side_effects=True, vmem_limit_bytes=60 * 1024 * 1024
         ),
-    )(mol_feats, w_src, w_dst, w_out.T, idx, idx_own, blocks, tails)
+    )(mol_feats, w_src, w_dst, w_out.T, idx, idx_own, blocks)
     if not fused:
         src_g, dst_g, out_g = [
             lax.psum_scatter(part, "space", scatter_dimension=0, tiled=True) for part in (src_g, dst_g, out_g)
         ]
-        return fgrad, src_g, dst_g, out_g
-    results = (fgrad, src_g, dst_g, out_g)
-    return pl.pallas_call(
-        write_out,
-        out_shape=tuple(jax.ShapeDtypeStruct(r.shape, r.dtype) for r in results),
-        in_specs=[near] * 4,
-        out_specs=(far,) * 4,
-        scratch_shapes=[dma((4,))],
-    )(*results)
+    return fgrad, src_g, dst_g, out_g
 
 
 def solution(mesh):

time: 89.6 us -> 71.2 us (0.79)
  Pallas kernels: 76.8 us -> 56.8 us
  local copies, waits for them, and re-layouts: 10.9 us -> 12.5 us
    pallas_call x1 -> x0, Pallas kernels: 23.5 us -> none  [on_device(): pl.pallas_call(write_out, out_shape=tuple((jax.ShapeDtypeStruct(r.shape,...]
    pallas_call x1, Pallas kernels: 53.4 us -> 56.8 us  [on_device(): pl.pallas_call(functools.partial(kernel, (n, half, mols, reach, factor, f...]
    unnamed x17 -> x5, local copies, waits for them, and re-layouts: 8.63 us -> 11.2 us
    reshape x2 -> x0, local copies, waits for them, and re-layouts: 1.98 us -> none  [on_device(): tails.reshape(n, pack, half // pack, tail_span).transpose(0, 2, 1, 3)]
where the time goes in v4:
time: 71.2 us; the launch traced here: 70.7 us
  Pallas kernels  56.8 us (80%)
  local copies, waits for them, and re-layouts  12.5 us (18%)
  other arithmetic  0.82 us (1%)
    pallas_call x1, Pallas kernels, on_device(): pl.pallas_call(functools.partial(kernel, (n, half, mols, reach, factor, f...  56.8 us
    unnamed x5, local copies, waits for them, and re-layouts  11.2 us

profile of v4, /device:TPU:0, one launch (start us, length us, event | category | flops | bytes accessed | tf_op | source)
XLA Modules:
  0.0 70.7 jit_solution(13304736318279704046)
XLA Ops:
  0.6 0.7 %fusion.3 = s32[16,128]{1,0:T(8,128)S(1)} fusion(s32[2048]{0:T(1024)} %param.14, s32[2048]{0:T(1024)} %param.13, s32[2048]{0:T(1024)} %param.15), kind=kLoop, calls=%fused_computation.4 | loop fusion | flops 20480 | bytes 32768 | tf_op jit(solution)/shard_map/reshape | solution.py:307
  1.4 0.5 constant_dynamic-slice_fusion.idx_own
  1.9 0.1 slice_select_fusion
  2.0 0.1 reshape.18
  2.1 0.7 reshape.19.idx
  2.8 4.8 %copy.13 = bf16[1,16,128,529]{3,2,1,0:T(8,128)(2,1)} copy(bf16[1,16,128,529]{2,1,3,0:T(8,128)(2,1)} %param.12) | data formatting | bytes 4333568 | tf_op args[4]
  7.6 56.8 %shard_map.111 = (f32[256,512]{1,0:T(8,128)}, f32[32,512]{1,0:T(8,128)}, f32[32,512]{1,0:T(8,128)}, f32[32,529]{1,0:T(8,128)}) custom-call(bf16[256,512]{1,0:T(8,128)(2,1)} %feats_far.1, bf16[512,512]{1,0:T(8,128)(2,1)} %w_src_far.1, bf16[512,512]{1,0:T(8,128)(2,1)} %w_dst_far.1, bf16[529,512]{1,0:T(8,128)(2,1)} %bitcast.6, s32[4,1,256]{2,1,0:T(1,128)} %reshape.19.idx, ...), custom_call_target="tpu_custom_call" | custom-call | tf_op jit(solution)/shard_map/pallas_call | solution.py:365
  64.4 1.9 %copy.18 = f32[256,512]{1,0:T(8,128)} copy(f32[256,512]{1,0:T(8,128)} %get-tuple-element.8) | data formatting | bytes 1048576
  66.3 1.5 %copy.19 = f32[32,512]{1,0:T(8,128)} copy(f32[32,512]{1,0:T(8,128)} %get-tuple-element.9) | data formatting | bytes 131072
  67.7 1.5 %copy.20 = f32[32,512]{1,0:T(8,128)} copy(f32[32,512]{1,0:T(8,128)} %get-tuple-element.10) | data formatting | bytes 131072
  69.2 1.5 %copy.21 = f32[32,529]{1,0:T(8,128)} copy(f32[32,529]{1,0:T(8,128)} %get-tuple-element.11) | data formatting | bytes 135424
  (2 shorter events, 0.0 us)
